TPU v7x, 128 devices: a whole 4x4x4 slice. The times are simulated.
128 devices in a mesh: patch: 8 (over z, x_lo), head: 16 (over x_hi, y, core).
Axes of the slice: x: 4 (x_hi: 2, x_lo: 2; x = x_hi * 2 + x_lo), y: 4, z: 4, core: 2. Of those that a mesh axis runs over, the one named last changes fastest.
Arguments:
- fresh_qkv: bfloat16 [16384, 3, 2048], P(('patch', 'head')), may hold values from -20 to 20
- stale_kv: bfloat16 [16384, 2, 2048], P(('patch', 'head')), may hold values from -20 to 20
- out_weight: bfloat16 [2048, 3072], replicated, may hold values from -0.375 to 0.375
Outputs:
- mixed: bfloat16 [16384, 3072], P(('patch', 'head'))
All inputs are finite; a program needn't handle non-finite values.
Results may differ from a plain program's by a relative error of at most 0.0095.
Values may be sent and summed in bfloat16 or wider, within the bound.
A program may use at most 128 MiB of HBM per device.

v0:
```python
import jax
import jax.numpy as jnp
from jax import lax
from jax.experimental import pallas as pl
from jax.experimental.pallas import tpu as pltpu
from jax.sharding import PartitionSpec as P

MESH = pl.DeviceIdType.MESH
BLK = 128
QUAD = 4 * BLK
QB = 512
MAX_KEYS = 1024
FACTOR = float(128 ** -0.5 * 1.4426950408889634)
F32 = jnp.float32
BF16 = jnp.bfloat16


def kernel(fresh, stale_in, weight, out,
           stale, keep, wbuf, send_s, send_f, kv, qbuf, acc_s, m_s, sbuf, po, pml, po_in, pml_in, a_out, a_in,
           in_sem, w_sem, q_send, q_recv, qx_send, qx_recv, s_send, s_recv, f_send, f_recv,
           up_send, up_recv, dn_send, dn_recv, up2_send, up2_recv, dn2_send, dn2_recv,
           po_send, po_recv, pml_send, pml_recv, a_send, a_recv):
    p, hd = lax.axis_index("patch"), lax.axis_index("head")
    z, xl = p // 2, p % 2
    xh, j = hd // 8, hd % 8
    yh, jl = j // 4, j % 4
    me = xl * 8 + j
    my_head = (xl + xh - 2 * xl * xh) * 8 + j
    above = (2 * ((z + 1) % 4) + xl, hd)
    below = (2 * ((z + 3) % 4) + xl, hd)
    partner = (2 * z + 1 - xl, (1 - xh) * 8 + j)
    TURN = ((1, 0), (0, 1), (1, 1), (0, 0))

    def side(k):
        return (xl + TURN[k][0]) % 2, (yh + TURN[k][1]) % 2

    def quad(plane, k):
        a, b = side(k)
        return (plane * 2 + a) * 2 + b

    def remote(src, dst, send, recv, to):
        return pltpu.make_async_remote_copy(
            src_ref=src, dst_ref=dst, send_sem=send, recv_sem=recv, device_id=to, device_id_type=MESH)

    def wait_bytes(ref, sem):
        pltpu.make_async_copy(ref, ref, sem).wait()

    def lane(h):
        return pl.ds(pl.multiple_of(h * BLK, BLK), BLK)

    def each_member(k, action):
        a, b = side(k)

        def one(d, c):
            tj = b * 4 + (jl + d) % 4
            action((2 * z + a, xh * 8 + tj), (a + xh - 2 * a * xh) * 8 + tj)
            return c

        lax.fori_loop(1 if k == 3 else 0, 4, one, 0)

    barrier = pltpu.get_barrier_semaphore()

    def greet(to, h):
        pl.semaphore_signal(barrier, inc=1, device_id=to, device_id_type=MESH)

    for k in range(4):
        each_member(k, greet)
    for to in (above, below, partner):
        greet(to, 0)

    weight_copy = pltpu.make_async_copy(weight, wbuf, w_sem)
    stale_copy = pltpu.make_async_copy(stale_in, stale, in_sem.at[0])
    fresh_copy = pltpu.make_async_copy(fresh.at[pl.ds(1, 2)], keep, in_sem.at[1])
    stale_copy.start()
    fresh_copy.start()
    stale_copy.wait()
    def pack_stale(k):
        a, b = side(k)
        for t in range(4):
            h = (a + xh - 2 * a * xh) * 8 + b * 4 + t
            pair = stale[:, :, lane(h)]
            send_s[h, 0] = pair[:, 0, :]
            send_s[h, 1] = pair[:, 1, :].T

    pack_stale(0)
    pack_stale(1)
    pl.semaphore_wait(barrier, 18)

    def send_stale(k):
        each_member(k, lambda to, h: remote(
            send_s.at[h], kv.at[quad(z, 3), jl], s_send, s_recv.at[k], to).start())

    send_stale(0)
    send_stale(1)
    for k in range(4):
        each_member(k, lambda to, h: remote(
            fresh.at[0, :, lane(h)], qbuf.at[0, xl, yh, jl], q_send, q_recv.at[k], to).start())
    pltpu.make_async_copy(fresh.at[0, :, lane(my_head)], qbuf.at[0, xl, yh, jl], q_recv.at[3]).start()

    def send_fresh(k):
        each_member(k, lambda to, h: remote(
            send_f.at[h], kv.at[16 + xl * 2 + yh, jl], f_send, f_recv, to).start())

    pack_stale(2)
    pack_stale(3)
    fresh_copy.wait()
    for h in range(16):
        cols = slice(h * BLK, (h + 1) * BLK)
        send_f[h, 0] = keep[0, :, cols]
        send_f[h, 1] = keep[1, :, cols].T

    def pass_queries(k):
        a, b = side(k)
        wait_bytes(qbuf.at[0, a, b], q_recv.at[k])
        remote(qbuf.at[0, a, b], qbuf.at[1, a, b], qx_send, qx_recv, partner).start()

    def stale_here(k):
        wait_bytes(kv.at[quad(z, k)], s_recv.at[k])

    def pass_stale(k):
        slot = kv.at[quad(z, k)]
        remote(slot, slot, up_send, up_recv.at[k], above).start()
        remote(slot, slot, dn_send, dn_recv.at[k], below).start()

    def stale_here(k):
        wait_bytes(kv.at[quad(z, k)], s_recv.at[k])

    def pass_stale(k):
        slot = kv.at[quad(z, k)]
        remote(slot, slot, up_send, up_recv.at[k], above).start()
        remote(slot, slot, dn_send, dn_recv.at[k], below).start()

    zb, za, zo = (z + 3) % 4, (z + 1) % 4, (z + 2) % 4

    def from_below(k):
        wait_bytes(kv.at[quad(zb, k)], up_recv.at[k])

    def from_above(k):
        wait_bytes(kv.at[quad(za, k)], dn_recv.at[k])

    def on_up(k):
        slot = kv.at[quad(zb, k)]
        remote(slot, slot, up2_send, up2_recv.at[k // 2], above).start()

    def on_down(k):
        slot = kv.at[quad(za, k)]
        remote(slot, slot, dn2_send, dn2_recv.at[k // 2], below).start()

    NEAR_0, NEAR_1, NEAR_2, NEAR_3, FAR_A, FAR_B, SAME, FRESH = range(8)
    OWN, OTHER = 0, 4
    ROUNDS = ((OWN, NEAR_0), (OWN, SAME), (OWN, NEAR_1), (OTHER, SAME), (OTHER, NEAR_0), (OTHER, NEAR_1),
              (OTHER, FRESH), (OTHER, NEAR_2), (OTHER, NEAR_3), (OTHER, FAR_A), (OTHER, FAR_B), (OWN, FRESH))
    N_ROUNDS = len(ROUNDS)
    LATE = (0, 1, 2, 3, 6, 9)

    def pick(index, values):
        out = values[0]
        for n in range(1, len(values)):
            out = jnp.where(index == n, values[n], out)
        return out

    def item(r, u):
        block = pick(r, [where for where, _ in ROUNDS]) + u
        kind = pick(r, [what for _, what in ROUNDS])
        patch = u // 2
        same = z * 2 + 1 - patch
        first = pick(kind, [quad(zb, k) for k in range(4)] + [quad(zo, 0), quad(zo, 2), same * 2, 16 + patch * 2])
        second = pick(kind, [quad(za, k) for k in range(4)] + [quad(zo, 1), quad(zo, 3), same * 2 + 1, 17 + patch * 2])
        return block, first, second

    def scores(block, first, second):
        keys = jnp.concatenate([kv[q4, :, 0].reshape(QUAD, BLK) for q4 in (first, second)], axis=0)
        queries = qbuf[block // 4, (block // 2) % 2, block % 2].reshape(QB, BLK)
        return lax.dot_general(keys, queries, (((1,), (1,)), ((), ())), preferred_element_type=F32)

    def settle(block, first, second, weights, shrink):
        values = jnp.concatenate([kv[q4, c, 1] for q4 in (first, second) for c in range(4)], axis=1)
        values = jnp.concatenate([values, jnp.ones((16, 2 * QUAD), BF16)], axis=0)
        acc_s[block] = acc_s[block] * shrink + jnp.dot(values, weights, preferred_element_type=F32)

    def before_round(r):
        @pl.when(r == 0)
        def _():
            from_below(0)
            from_above(0)

        @pl.when(r == 1)
        def _():
            stale_here(2)
            pass_stale(2)
            stale_here(3)
            pass_stale(3)
            for k in range(4):
                send_fresh(k)
            pltpu.make_async_copy(send_f.at[my_head], kv.at[16 + xl * 2 + yh, jl], f_recv).start()
            weight_copy.start()
            on_up(0)

        @pl.when(r == 2)
        def _():
            from_above(1)
            on_down(1)
            from_below(1)

        @pl.when(r == 3)
        def _():
            wait_bytes(qbuf.at[1], qx_recv)

        @pl.when(r == 6)
        def _():
            from_below(2)
            on_up(2)
            from_above(3)
            on_down(3)
            from_above(2)
            from_below(3)
            wait_bytes(kv.at[pl.ds(16, 4)], f_recv)

        @pl.when(r == 9)
        def _():
            wait_bytes(kv.at[quad(zo, 0)], up2_recv.at[0])
            wait_bytes(kv.at[quad(zo, 1)], dn2_recv.at[0])
            wait_bytes(kv.at[quad(zo, 2)], up2_recv.at[1])
            wait_bytes(kv.at[quad(zo, 3)], dn2_recv.at[1])

    def any_of(r, values):
        found = r == values[0]
        for v in values[1:]:
            found = jnp.logical_or(found, r == v)
        return found

    def hand_over(i, c):
        block = (((1 - xl) * 2 + yh + 1 + i) % 4)
        acc, m = acc_s[4 + block], m_s[4 + block, 0:1]
        l = acc[BLK:BLK + 1]
        po[block] = (acc[:BLK] * (1.0 / l)).astype(BF16)
        pml[block, 0:4] = jnp.broadcast_to(m, (4, QB))
        pml[block, 4:8] = jnp.broadcast_to(l, (4, QB))
        remote(po.at[block], po_in.at[block], po_send.at[block], po_recv.at[block], partner).start()
        remote(pml.at[block], pml_in.at[block], pml_send.at[block], pml_recv.at[block], partner).start()
        return c

    def combine(qb, m, l, acc):
        wait_bytes(po_in.at[qb], po_recv.at[qb])
        wait_bytes(pml_in.at[qb], pml_recv.at[qb])
        m2, l2 = pml_in[qb, 0:1], pml_in[qb, 4:5]
        top = jnp.maximum(m, m2)
        mine, other = jnp.exp2(m - top), jnp.exp2(m2 - top) * l2
        scale = 1.0 / (l * mine + other)
        both = acc * (mine * scale) + po_in[qb].astype(F32) * (other * scale)
        a_out[qb] = both.astype(BF16).T.reshape(4, BLK, BLK)

        for d in range(4):
            t = (jl + d) % 4
            if d == 0 and len(combined) == 3:
                pltpu.make_async_copy(a_out.at[qb, t], a_in.at[my_head], a_recv).start()
            else:
                remote(a_out.at[qb, t], a_in.at[my_head], a_send, a_recv,
                       (2 * z + qb // 2, xh * 8 + (qb % 2) * 4 + t)).start()
        combined.append(qb)

    combined = []
    def one_round(r, c):
        before_round(r)
        items = [item(r, u) for u in range(4)]
        ahead_r = jnp.where(jnp.logical_or(any_of(r, [v - 1 for v in LATE[1:]]), r == N_ROUNDS - 1), r, r + 1)
        following = item(ahead_r, 0)

        @pl.when(any_of(r, LATE))
        def _():
            sbuf[...] = scores(*items[0])

        s = sbuf[...]
        behind = None
        for u in range(4):
            if u < 3:
                upcoming = scores(*items[u + 1])
            else:
                sbuf[...] = scores(*following)
            if behind is not None:
                settle(*behind)
            block = items[u][0]
            before = m_s[block, 0:1]
            m = jnp.maximum(before, jnp.max(s, axis=0, keepdims=True) * FACTOR)
            m_s[block, 0:1] = m
            behind = (*items[u], jnp.exp2(s * FACTOR - m).astype(BF16), jnp.exp2(before - m))
            if u < 3:
                s = upcoming
        settle(*behind)

        @pl.when(r == 10)
        def _():
            lax.fori_loop(0, 4, hand_over, 0)

        return c

    m_s[...] = jnp.full(m_s.shape, -1e30, F32)
    acc_s[...] = jnp.zeros(acc_s.shape, F32)
    stale_here(0)
    pass_stale(0)
    stale_here(1)
    pass_stale(1)
    pass_queries(0)
    pass_queries(1)
    send_stale(2)
    send_stale(3)
    pltpu.make_async_copy(send_s.at[my_head], kv.at[quad(z, 3), jl], s_recv.at[3]).start()
    pass_queries(2)
    pass_queries(3)
    lax.fori_loop(0, N_ROUNDS, one_round, 0)

    steps = [(quad(zb, 2), quad(za, 2)), (quad(zb, 3), quad(za, 3)),
             (quad(zo, 0), quad(zo, 1)), (quad(zo, 2), quad(zo, 3))]
    blocks = [(xl * 2 + yh + 1 + i) % 4 for i in range(4)]
    s = scores(blocks[0], *steps[0])
    behind = None

    def weigh(behind):
        first, second, w, shrink, acc = behind
        values = jnp.concatenate([kv[q4, c, 1] for q4 in (first, second) for c in range(4)], axis=1)
        values = jnp.concatenate([values, jnp.ones((16, 2 * QUAD), BF16)], axis=0)
        return acc * shrink + jnp.dot(values, w, preferred_element_type=F32)

    for i in range(4):
        for n in range(4):
            if n < 3:
                upcoming = scores(blocks[i], *steps[n + 1])
            elif i < 3:
                upcoming = scores(blocks[i + 1], *steps[0])
            if n == 0:
                before, acc = m_s[blocks[i], 0:1], acc_s[blocks[i]]
            else:
                before = m
            if behind is not None:
                done = weigh(behind)
                if n == 0:
                    combine(blocks[i - 1], m, done[BLK:BLK + 1], done[:BLK])
                else:
                    acc = done
            m = jnp.maximum(before, jnp.max(s, axis=0, keepdims=True) * FACTOR)
            behind = (*steps[n], jnp.exp2(s * FACTOR - m).astype(BF16), jnp.exp2(before - m), acc)
            s = upcoming
    done = weigh(behind)
    combine(blocks[3], m, done[BLK:BLK + 1], done[:BLK])

    weight_copy.wait()
    wait_bytes(a_in, a_recv)
    rows = jnp.concatenate([a_in[h] for h in range(16)], axis=1)

    def project(n, c):
        cols = pl.ds(pl.multiple_of(n * 512, 512), 512)
        out[:, cols] = jnp.dot(rows, wbuf[:, cols], preferred_element_type=F32).astype(BF16)
        return c

    lax.fori_loop(0, 6, project, 0)

    wait_bytes(qbuf.at[0], qx_send)
    wait_bytes(kv.at[pl.ds(0, 4)], up_send)
    wait_bytes(kv.at[pl.ds(0, 4)], dn_send)
    wait_bytes(kv.at[pl.ds(0, 2)], up2_send)
    wait_bytes(kv.at[pl.ds(0, 2)], dn2_send)
    wait_bytes(a_in.at[pl.ds(0, 15)], q_send)
    wait_bytes(a_in.at[pl.ds(0, 15)], a_send)
    wait_bytes(send_s.at[pl.ds(0, 15)], s_send)
    wait_bytes(send_s.at[pl.ds(0, 15)], f_send)
    for pb in range(4):
        wait_bytes(po.at[pb], po_send.at[pb])
        wait_bytes(pml.at[pb], pml_send.at[pb])


def on_device(fresh_qkv, stale_kv, out_weight):
    fresh, stale = jnp.transpose(fresh_qkv, (1, 0, 2)), stale_kv
    vmem = pl.BlockSpec(memory_space=pltpu.VMEM)
    dma = pltpu.SemaphoreType.DMA
    rows, width = fresh.shape[1], out_weight.shape[1]
    return pl.pallas_call(
        kernel,
        out_shape=jax.ShapeDtypeStruct((rows, width), BF16),
        in_specs=[pl.BlockSpec(memory_space=pl.ANY)] * 3,
        out_specs=vmem,
        scratch_shapes=[
            pltpu.VMEM(stale.shape, BF16),
            pltpu.VMEM((2,) + fresh.shape[1:], BF16),
            pltpu.VMEM(out_weight.shape, BF16),
            pltpu.VMEM((16, 2, BLK, BLK), BF16),
            pltpu.VMEM((16, 2, BLK, BLK), BF16),
            pltpu.VMEM((20, 4, 2, BLK, BLK), BF16),
            pltpu.VMEM((2, 2, 2, 4, BLK, BLK), BF16),
            pltpu.VMEM((8, BLK + 16, QB), F32),
            pltpu.VMEM((8, 8, QB), F32),
            pltpu.VMEM((MAX_KEYS, QB), F32),
            pltpu.VMEM((4, BLK, QB), BF16),
            pltpu.VMEM((4, 8, QB), F32),
            pltpu.VMEM((4, BLK, QB), BF16),
            pltpu.VMEM((4, 8, QB), F32),
            pltpu.VMEM((4, 4, BLK, BLK), BF16),
            pltpu.VMEM((16, BLK, BLK), BF16),
            dma((2,)), dma, dma, dma((4,)), dma, dma, dma, dma((4,)), dma, dma,
            dma, dma((4,)), dma, dma((4,)), dma, dma((2,)), dma, dma((2,)),
            dma((4,)), dma((4,)), dma((4,)), dma((4,)), dma, dma,
        ],
        compiler_params=pltpu.CompilerParams(
            collective_id=0, has_side_effects=True, vmem_limit_bytes=60 * 2 ** 20),
        cost_estimate=pl.CostEstimate(flops=19 * 10 ** 9, bytes_accessed=16 * 2 ** 20, transcendentals=2 ** 25),
    )(fresh, stale, out_weight)


def solution(mesh):
    return jax.shard_map(
        on_device,
        mesh=mesh,
        in_specs=(P(("patch", "head"), None, None), P(("patch", "head"), None, None), P()),
        out_specs=P(("patch", "head"), None),
        check_vma=False,
    )
```

profile of v0, /device:TPU:1, one launch (start us, length us, event | category | flops | bytes accessed | tf_op | source)
XLA Modules:
  0.0 83.0 jit_solution(12568389493773730671)
XLA Ops:
  0.0 80.9 %shard_map.37 = bf16[128,3072]{1,0:T(8,128)(2,1)} custom-call(bf16[3,128,2048]{2,1,0:T(8,128)(2,1)} %bitcast.1, bf16[128,2,2048]{2,1,0:T(2,128)(2,1)} %stale_in.1, bf16[2048,3072]{1,0:T(8,128)(2,1)} %weight.1), custom_call_target="tpu_custom_call" | custom-call | flops 19000000512 | bytes 16777216 | tf_op jit(solution)/shard_map/pallas_call | solution.py:376
  81.0 2.1 %copy.5 = bf16[128,3072]{1,0:T(8,128)(2,1)} copy(bf16[128,3072]{1,0:T(8,128)(2,1)} %shard_map.37) | data formatting | bytes 1572864
where the time goes:
time: 83.2 us; the launch traced here: 83 us
  Pallas kernels  80.9 us (97%)
  local copies, waits for them, and re-layouts  2.06 us (2%)
    pallas_call x1, Pallas kernels, on_device(): pl.pallas_call(kernel, out_shape=jax.ShapeDtypeStruct((rows, width), BF16...  80.9 us
    unnamed x1, local copies, waits for them, and re-layouts  2.06 us

commit v1 on v0

--- a/solution.py
+++ b/solution.py
@@ -15,9 +15,9 @@
 BF16 = jnp.bfloat16
 
 
-def kernel(fresh, stale_in, weight, out,
-           stale, keep, wbuf, send_s, send_f, kv, qbuf, acc_s, m_s, sbuf, po, pml, po_in, pml_in, a_out, a_in,
-           in_sem, w_sem, q_send, q_recv, qx_send, qx_recv, s_send, s_recv, f_send, f_recv,
+def kernel(fresh, stale, out,
+           send_s, send_f, kv, qbuf, acc_s, m_s, sbuf, po, pml, po_in, pml_in, a_out, a_in,
+           q_send, q_recv, qx_send, qx_recv, s_send, s_recv, f_send, f_recv,
            up_send, up_recv, dn_send, dn_recv, up2_send, up2_recv, dn2_send, dn2_recv,
            po_send, po_recv, pml_send, pml_recv, a_send, a_recv):
     p, hd = lax.axis_index("patch"), lax.axis_index("head")
@@ -68,12 +68,6 @@
     for to in (above, below, partner):
         greet(to, 0)
 
-    weight_copy = pltpu.make_async_copy(weight, wbuf, w_sem)
-    stale_copy = pltpu.make_async_copy(stale_in, stale, in_sem.at[0])
-    fresh_copy = pltpu.make_async_copy(fresh.at[pl.ds(1, 2)], keep, in_sem.at[1])
-    stale_copy.start()
-    fresh_copy.start()
-    stale_copy.wait()
     def pack_stale(k):
         a, b = side(k)
         for t in range(4):
@@ -103,11 +97,10 @@
 
     pack_stale(2)
     pack_stale(3)
-    fresh_copy.wait()
     for h in range(16):
         cols = slice(h * BLK, (h + 1) * BLK)
-        send_f[h, 0] = keep[0, :, cols]
-        send_f[h, 1] = keep[1, :, cols].T
+        send_f[h, 0] = fresh[1, :, cols]
+        send_f[h, 1] = fresh[2, :, cols].T
 
     def pass_queries(k):
         a, b = side(k)
@@ -193,7 +186,6 @@
             for k in range(4):
                 send_fresh(k)
             pltpu.make_async_copy(send_f.at[my_head], kv.at[16 + xl * 2 + yh, jl], f_recv).start()
-            weight_copy.start()
             on_up(0)
 
         @pl.when(r == 2)
@@ -300,11 +292,11 @@
     pass_stale(0)
     stale_here(1)
     pass_stale(1)
-    pass_queries(0)
-    pass_queries(1)
     send_stale(2)
     send_stale(3)
     pltpu.make_async_copy(send_s.at[my_head], kv.at[quad(z, 3), jl], s_recv.at[3]).start()
+    pass_queries(0)
+    pass_queries(1)
     pass_queries(2)
     pass_queries(3)
     lax.fori_loop(0, N_ROUNDS, one_round, 0)
@@ -343,16 +335,9 @@
     done = weigh(behind)
     combine(blocks[3], m, done[BLK:BLK + 1], done[:BLK])
 
-    weight_copy.wait()
     wait_bytes(a_in, a_recv)
-    rows = jnp.concatenate([a_in[h] for h in range(16)], axis=1)
-
-    def project(n, c):
-        cols = pl.ds(pl.multiple_of(n * 512, 512), 512)
-        out[:, cols] = jnp.dot(rows, wbuf[:, cols], preferred_element_type=F32).astype(BF16)
-        return c
-
-    lax.fori_loop(0, 6, project, 0)
+    for h in range(16):
+        out[:, h * BLK:(h + 1) * BLK] = a_in[h]
 
     wait_bytes(qbuf.at[0], qx_send)
     wait_bytes(kv.at[pl.ds(0, 4)], up_send)
@@ -372,16 +357,13 @@
     fresh, stale = jnp.transpose(fresh_qkv, (1, 0, 2)), stale_kv
     vmem = pl.BlockSpec(memory_space=pltpu.VMEM)
     dma = pltpu.SemaphoreType.DMA
-    rows, width = fresh.shape[1], out_weight.shape[1]
-    return pl.pallas_call(
+    rows = fresh.shape[1]
+    attended = pl.pallas_call(
         kernel,
-        out_shape=jax.ShapeDtypeStruct((rows, width), BF16),
-        in_specs=[pl.BlockSpec(memory_space=pl.ANY)] * 3,
+        out_shape=jax.ShapeDtypeStruct((rows, out_weight.shape[0]), BF16),
+        in_specs=[vmem] * 2,
         out_specs=vmem,
         scratch_shapes=[
-            pltpu.VMEM(stale.shape, BF16),
-            pltpu.VMEM((2,) + fresh.shape[1:], BF16),
-            pltpu.VMEM(out_weight.shape, BF16),
             pltpu.VMEM((16, 2, BLK, BLK), BF16),
             pltpu.VMEM((16, 2, BLK, BLK), BF16),
             pltpu.VMEM((20, 4, 2, BLK, BLK), BF16),
@@ -395,14 +377,15 @@
             pltpu.VMEM((4, 8, QB), F32),
             pltpu.VMEM((4, 4, BLK, BLK), BF16),
             pltpu.VMEM((16, BLK, BLK), BF16),
-            dma((2,)), dma, dma, dma((4,)), dma, dma, dma, dma((4,)), dma, dma,
+            dma, dma((4,)), dma, dma, dma, dma((4,)), dma, dma,
             dma, dma((4,)), dma, dma((4,)), dma, dma((2,)), dma, dma((2,)),
             dma((4,)), dma((4,)), dma((4,)), dma((4,)), dma, dma,
         ],
         compiler_params=pltpu.CompilerParams(
-            collective_id=0, has_side_effects=True, vmem_limit_bytes=60 * 2 ** 20),
+            collective_id=0, has_side_effects=True, vmem_limit_bytes=38 * 2 ** 20),
         cost_estimate=pl.CostEstimate(flops=19 * 10 ** 9, bytes_accessed=16 * 2 ** 20, transcendentals=2 ** 25),
-    )(fresh, stale, out_weight)
+    )(fresh, stale)
+    return jnp.dot(attended, out_weight, preferred_element_type=F32).astype(BF16)
 
 
 def solution(mesh):

time: 83.2 us -> 82.7 us (level)
  Pallas kernels: 80.9 us -> 77.2 us
  matrix products: 0 us -> 2.68 us
    pallas_call x1, Pallas kernels: 80.9 us -> 77.2 us  [on_device(): pl.pallas_call(kernel, out_shape=jax.ShapeDtypeStruct((rows, out_weight.s...]
    dot_general x0 -> x1, matrix products: none -> 2.68 us  [on_device(): jnp.dot(attended, out_weight, preferred_element_type=F32).astype(BF16)]
    unnamed x1 -> x6, local copies, waits for them, and re-layouts: 2.06 us -> 2.64 us
where the time goes in v1:
time: 82.7 us; the launch traced here: 82.5 us
  Pallas kernels  77.2 us (93%)
  matrix products  2.68 us (3%)
  local copies, waits for them, and re-layouts  2.64 us (3%)
    pallas_call x1, Pallas kernels, on_device(): pl.pallas_call(kernel, out_shape=jax.ShapeDtypeStruct((rows, out_weight.s...  77.2 us
    dot_general x1, matrix products, on_device(): jnp.dot(attended, out_weight, preferred_element_type=F32).astype(BF16)  2.68 us
    unnamed x6, local copies, waits for them, and re-layouts  2.64 us

profile of v1, /device:TPU:1, one launch (start us, length us, event | category | flops | bytes accessed | tf_op | source)
XLA Modules:
  0.0 82.5 jit_solution(5845377190244991602)
XLA Ops:
  0.0 0.0 copy-start
  0.0 1.4 %copy-done = bf16[128,3,2048]{2,0,1:T(8,128)(2,1)S(1)} copy-done((bf16[128,3,2048]{2,0,1:T(8,128)(2,1)S(1)}, bf16[128,3,2048]{2,0,1:T(8,128)(2,1)}, u32[]{:S(2)}) %copy-start) | copy-done | bytes 1572888
  1.4 0.0 copy-start.1
  1.4 1.2 %copy-done.1 = bf16[128,2,2048]{2,1,0:T(2,128)(2,1)S(1)} copy-done((bf16[128,2,2048]{2,1,0:T(2,128)(2,1)S(1)}, bf16[128,2,2048]{2,1,0:T(2,128)(2,1)}, u32[]{:S(2)}) %copy-start.1) | copy-done | bytes 1048600
  2.6 0.0 copy-start.2
  2.6 77.2 %shard_map.37 = bf16[128,2048]{1,0:T(8,128)(2,1)S(1)} custom-call(bf16[3,128,2048]{2,1,0:T(8,128)(2,1)S(1)} %bitcast.3, bf16[128,2,2048]{2,1,0:T(2,128)(2,1)S(1)} %copy-done.1), custom_call_target="tpu_custom_call" | custom-call | flops 19000000512 | bytes 16777216 | tf_op jit(solution)/shard_map/pallas_call | solution.py:361
  79.8 0.0 copy-done.2
  79.8 2.7 %convolution_convert_fusion = bf16[128,3072]{1,0:T(8,128)(2,1)} fusion(bf16[128,2048]{1,0:T(8,128)(2,1)S(1)} %shard_map.37, bf16[2048,3072]{1,0:T(8,128)(2,1)S(1)} %copy-done.2), kind=kOutput, calls=%fused_computation | convolution fusion | flops 1611005952 | bytes 13893632 | tf_op jit(solution)/shard_map/dot_general | solution.py:388
Async XLA Ops:
  0.0 1.4 %copy-start = (bf16[128,3,2048]{2,0,1:T(8,128)(2,1)S(1)}, bf16[128,3,2048]{2,0,1:T(8,128)(2,1)}, u32[]{:S(2)}) copy-start(bf16[128,3,2048]{2,0,1:T(8,128)(2,1)} %param.3) | copy-start | bytes 4718596
  1.4 1.2 %copy-start.1 = (bf16[128,2,2048]{2,1,0:T(2,128)(2,1)S(1)}, bf16[128,2,2048]{2,1,0:T(2,128)(2,1)}, u32[]{:S(2)}) copy-start(bf16[128,2,2048]{2,1,0:T(2,128)(2,1)} %stale.1) | copy-start | bytes 3145732
  2.6 77.2 %copy-start.2 = (bf16[2048,3072]{1,0:T(8,128)(2,1)S(1)}, bf16[2048,3072]{1,0:T(8,128)(2,1)}, u32[]{:S(2)}) copy-start(bf16[2048,3072]{1,0:T(8,128)(2,1)} %param.5) | copy-start | bytes 37748740
